TPU v7x, 32 devices: a whole 2x2x4 slice. The times are simulated.
32 devices in a mesh: row: 4 (over x, core), col: 8 (over z, y).
Axes of the slice: x: 2, y: 2, z: 4, core: 2. Of those that a mesh axis runs over, the one named last changes fastest.
Arguments:
- velocity: float32 [3, 1536, 32, 1536], P(None, 'col', None, 'row'), may hold values from -6 to 6
- wall_operator: bfloat16 [1536, 1536], replicated, may hold values from -0.15625 to 0.15625
- span_operator: bfloat16 [1536, 1536], replicated, may hold values from -0.15625 to 0.15625
Outputs:
- convection: float32 [3, 1536, 32, 1536], P(None, 'col', None, 'row')
All inputs are finite; a program needn't handle non-finite values.
Results may differ from a plain program's by a relative error of at most 0.0053.
Values may be sent and summed in bfloat16 or wider, within the bound.
A program may use at most 320 MiB of HBM per device.

v0:
```python
import jax
import jax.numpy as jnp
from jax import lax
from jax.sharding import PartitionSpec as P


def skew_terms(slope_list, speed_field_holder):
    return jnp.stack(
        [
            0.5 * (slope_list[3 + index] + speed_field_holder * slope_list[index])
            for index in range(3)
        ],
        0,
    )


def wall_terms(wall_rows, wall_operator):
    speed_field_holder = wall_rows[1].astype(jnp.float32)
    speed_pair_flux = (wall_rows.astype(jnp.float32) * speed_field_holder).astype(jnp.bfloat16)
    stacked = jnp.concatenate([wall_rows, speed_pair_flux], 0)
    gradient_entries = jnp.einsum(
        "fry,Yy->frY", stacked, wall_operator, preferred_element_type=jnp.float32
    )
    return skew_terms([gradient_entries[index] for index in range(6)], speed_field_holder)


def span_terms(span_lines, span_operator):
    merged = span_lines.reshape(3, span_lines.shape[1], span_lines.shape[2] * span_lines.shape[3])
    speed_field_holder = merged[2].astype(jnp.float32)
    speed_pair_flux = (merged.astype(jnp.float32) * speed_field_holder).astype(jnp.bfloat16)
    fields = [merged[index] for index in range(3)] + [speed_pair_flux[index] for index in range(3)]
    slope_list = [
        jnp.dot(span_operator, field, preferred_element_type=jnp.float32) for field in fields
    ]
    return skew_terms(slope_list, speed_field_holder).reshape(span_lines.shape)


def body(velocity, wall_operator, span_operator):
    truncated_outcome = velocity.astype(jnp.bfloat16)
    wall_lines = lax.all_to_all(truncated_outcome, "row", split_axis=2, concat_axis=3, tiled=True)
    span_local = wall_lines.shape[1]
    plane_local = wall_lines.shape[2]
    wall_cells = wall_lines.shape[3]
    wall_rows = wall_lines.reshape(3, span_local * plane_local, wall_cells)
    wall_part = wall_terms(wall_rows, wall_operator).reshape(wall_lines.shape)
    span_lines = lax.all_to_all(wall_lines, "col", split_axis=3, concat_axis=1, tiled=True)
    span_back = lax.all_to_all(
        span_terms(span_lines, span_operator), "col", split_axis=1, concat_axis=3, tiled=True
    )
    combined = wall_part + span_back
    return lax.all_to_all(combined, "row", split_axis=3, concat_axis=2, tiled=True)


def solution(mesh):
    placed = (P(None, "col", None, "row"), P(), P())
    return jax.shard_map(
        body, mesh=mesh, in_specs=placed, out_specs=P(None, "col", None, "row"), check_vma=False
    )
```

profile of v0, /device:TPU:30, one launch (start us, length us, event | category | flops | bytes accessed | tf_op | source)
XLA Modules:
  0.0 2379.8 jit_solution(16945710372112254181)
XLA Ops:
  0.0 14.7 copy.50
  14.7 158.0 %all_to_all.69 = bf16[3,192,32,384]{3,1,0,2:T(8,128)(2,1)} all-to-all(bf16[3,192,32,384]{3,1,0,2:T(8,128)(2,1)S(1)} %copy.50), channel_id=1, replica_groups=mesh['row'=4,'col'=8] {'row'}, dimensions={2} | all-to-all | bytes 28311552 | tf_op jit(solution)/shard_map/all_to_all | solution.py:40
  172.7 25.7 %copy.33 = bf16[3,192,8,4,384]{1,2,0,4,3:T(8,128)(2,1)} copy(bf16[3,192,8,4,384]{4,1,0,2,3:T(8,128)(2,1)} %bitcast.77) | data formatting | bytes 28311552 | tf_op jit(solution)/shard_map/all_to_all | solution.py:40
  198.3 414.2 %all_to_all.70 = bf16[3,192,8,1536]{1,2,0,3:T(8,128)(2,1)} all-to-all(bf16[3,192,8,1536]{1,2,0,3:T(8,128)(2,1)} %bitcast.85), channel_id=1, replica_groups=mesh['row'=4,'col'=8] {'col'}, dimensions={3} | all-to-all | bytes 28311552 | tf_op jit(solution)/shard_map/all_to_all | solution.py:46
  612.5 76.6 %copy.47 = bf16[3,192,8,8,192]{4,3,2,1,0:T(8,128)(2,1)} copy(bf16[3,192,8,8,192]{1,2,0,4,3:T(8,128)(2,1)} %bitcast.84) | data formatting | bytes 28311552 | tf_op jit(solution)/shard_map/all_to_all | solution.py:46
  689.1 21.6 bitcast_convert_fusion
  710.6 3.9 copy-done
  714.5 6.7 fusion.18
  721.2 11.7 copy.36
  732.9 10.6 squeeze.12
  743.5 7.4 copy.37
  750.9 35.9 %copy.35 = f32[3,8,192,8,192]{4,3,2,1,0:T(8,128)} copy(f32[3,8,192,8,192]{4,1,3,2,0:T(8,128)} %bitcast_convert_fusion) | data formatting | bytes 56623104 | tf_op jit(solution)/shard_map/convert_element_type | solution.py:30
  786.8 37.5 %reshape.53 = f32[3,1536,1536]{2,1,0:T(8,128)} reshape(f32[3,8,192,8,192]{4,3,2,1,0:T(8,128)} %copy.35) | data formatting | bytes 56623104 | tf_op jit(solution)/shard_map/convert_element_type | solution.py:30
  824.2 6.8 copy.38
  831.0 10.6 squeeze.28
  841.6 13.9 convolution_multiply_fusion
  855.5 0.0 slice-done.3
  855.5 0.0 slice-start.2
  855.6 0.0 slice-start.5
  855.6 13.1 convolution_multiply_fusion.2
  868.7 0.0 slice-start.6
  868.7 17.4 multiply_convert_fusion
  886.1 13.4 fusion.15
  899.5 12.8 copy.40
  912.2 6.8 copy.39
  919.0 10.6 squeeze.30
  929.6 13.6 convolution_multiply_fusion.1
  943.3 11.7 fusion.14
  955.0 12.8 copy.41
  967.8 14.6 fusion.13
  982.3 12.9 copy.42
  995.2 26.9 %pad_maximum_fusion = f32[3,1536,8,192]{3,2,0,1:T(8,128)} fusion(f32[1,1536,8,192]{3,2,0,1:T(8,128)} %copy.42, f32[1,1536,8,192]{3,2,0,1:T(8,128)} %copy.41, f32[1,1536,8,192]{3,2,0,1:T(8,128)} %copy.40), kind=kLoop, calls=%fused_computation | loop fusion | flops 14155776 | bytes 56623104 | tf_op jit(solution)/shard_map/stack | solution.py:8
  1022.1 10.0 all-to-all-start.2
  1032.1 21.5 copy.52
  1053.7 0.0 slice-start.9
  1053.7 1.3 slice_convert_fusion
  1055.1 4.8 copy-done.2
  1059.9 7.1 multiply_convert_fusion.1
  1067.0 0.2 copy-done.1
  1067.2 50.8 %fusion = f32[6,1536,1536]{2,1,0:T(8,128)} fusion(bf16[3,1536,1536]{2,1,0:T(8,128)(2,1)} %multiply_convert_fusion.1, bf16[3,1536,1536]{2,1,0:T(8,128)(2,1)} %bitcast.83, bf16[1536,1536]{1,0:T(8,128)(2,1)S(1)} %bitcast.98), kind=kOutput, calls=%fused_computation.2 | convolution fusion | flops 43500699648 | bytes 89653248 | tf_op jit(solution)/shard_map/fry,Yy->frY/dot_general | solution.py:21
  1118.0 32.5 %fusion.12 = (f32[1,192,8,1536]{3,2,1,0:T(8,128)}, f32[1,192,8,1536]{3,2,1,0:T(8,128)}, f32[1,192,8,1536]{3,2,1,0:T(8,128)}) fusion(f32[1,1536,1536]{2,1,0:T(8,128)} %bitcast.80, f32[6,1536,1536]{2,1,0:T(8,128)} %fusion), kind=kLoop, calls=%fused_computation.24 | loop fusion | flops 21233664 | bytes 94371840 | tf_op jit(solution)/shard_map/stack | solution.py:8
  1150.5 21.3 pad_maximum_fusion.1
  1171.7 37.4 %copy.44 = f32[3,192,8,1536]{1,2,0,3:T(8,128)} copy(f32[3,192,8,1536]{3,2,1,0:T(8,128)} %pad_maximum_fusion.1) | data formatting | bytes 56623104 | tf_op jit(solution)/shard_map/stack | solution.py:8
  1209.1 632.8 %all-to-all-done.2 = f32[3,1536,8,192]{3,2,0,1:T(8,128)} async-done(((f32[3,1536,8,192]{3,2,0,1:T(8,128)}), f32[3,1536,8,192]{3,2,0,1:T(8,128)}, u32[]{:S(2)}, u32[]{:S(2)}) %all-to-all-start.2) | async-done | bytes 28311584 | tf_op jit(solution)/shard_map/all_to_all | solution.py:47
  1841.9 39.4 %copy.43 = f32[3,192,8,8,192]{1,2,0,4,3:T(8,128)} copy(f32[3,192,8,8,192]{4,2,0,1,3:T(8,128)} %bitcast.24) | data formatting | bytes 56623104 | tf_op jit(solution)/shard_map/all_to_all | solution.py:47
  1881.3 37.7 %bitcast_add_fusion = f32[3,192,8,1536]{1,2,0,3:T(8,128)} fusion(f32[3,192,8,1536]{1,2,0,3:T(8,128)} %copy.44, f32[3,192,8,8,192]{1,2,0,4,3:T(8,128)} %copy.43), kind=kLoop, calls=%fused_computation.1 | loop fusion | flops 7077888 | bytes 84934656 | tf_op jit(solution)/shard_map/add | solution.py:50
  1919.1 426.5 %all_to_all.71 = f32[3,192,8,1536]{1,2,0,3:T(8,128)} all-to-all(f32[3,192,8,1536]{1,2,0,3:T(8,128)} %bitcast_add_fusion), channel_id=1, replica_groups=mesh['row'=4,'col'=8] {'row'}, dimensions={3} | all-to-all | bytes 56623104 | tf_op jit(solution)/shard_map/all_to_all | solution.py:51
  2345.6 34.0 %copy.45 = f32[3,192,4,8,384]{4,3,2,1,0:T(8,128)} copy(f32[3,192,4,8,384]{1,3,0,4,2:T(8,128)} %bitcast.76) | data formatting | bytes 56623104 | tf_op jit(solution)/shard_map/all_to_all | solution.py:51
  (25 shorter events, 0.0 us)
Async XLA Ops:
  689.1 25.4 %copy-start = (bf16[3,192,8,8,192]{4,3,2,1,0:T(8,128)(2,1)S(1)}, bf16[3,192,8,8,192]{4,3,2,1,0:T(8,128)(2,1)}, u32[]{:S(2)}) copy-start(bf16[3,192,8,8,192]{4,3,2,1,0:T(8,128)(2,1)} %copy.47) | copy-start | bytes 42467332
  831.0 24.5 %slice-start.3 = ((s8[4718592]{0:T(1024)(128)(4,1)}), s8[524288]{0:T(1024)(128)(4,1)S(1)}, s32[]{:S(2)}) async-start(s8[4718592]{0:T(1024)(128)(4,1)} %bitcast.88), calls=%async_computation.7 | async-start | bytes 1048576
  841.6 13.9 slice-start.4
  841.6 27.1 %slice-start = ((s8[9437184]{0:T(1024)(128)(4,1)}), s8[4194304]{0:T(1024)(128)(4,1)S(1)}, s32[]{:S(2)}) async-start(s8[9437184]{0:T(1024)(128)(4,1)} %bitcast.86), calls=%async_computation.4 | async-start | bytes 8388608
  841.6 27.1 %slice-start.1 = ((s8[9437184]{0:T(1024)(128)(4,1)}), s8[4194304]{0:T(1024)(128)(4,1)S(1)}, s32[]{:S(2)}) async-start(s8[9437184]{0:T(1024)(128)(4,1)} %bitcast.86), calls=%async_computation.5 | async-start | bytes 8388608
  855.5 13.1 slice-start.2
  855.6 30.5 %slice-start.5 = ((s8[4718592]{0:T(1024)(128)(4,1)}), s8[524288]{0:T(1024)(128)(4,1)S(1)}, s32[]{:S(2)}) async-start(s8[4718592]{0:T(1024)(128)(4,1)} %bitcast.93), calls=%async_computation.9 | async-start | bytes 1048576
  868.7 17.4 slice-start.6
  919.0 24.3 %slice-start.7 = ((s8[4718592]{0:T(1024)(128)(4,1)}), s8[524288]{0:T(1024)(128)(4,1)S(1)}, s32[]{:S(2)}) async-start(s8[4718592]{0:T(1024)(128)(4,1)} %bitcast.95), calls=%async_computation.11 | async-start | bytes 1048576
  929.6 13.7 slice-start.8
  1022.1 819.8 %all-to-all-start.2 = ((f32[3,1536,8,192]{3,2,0,1:T(8,128)}), f32[3,1536,8,192]{3,2,0,1:T(8,128)}, u32[]{:S(2)}, u32[]{:S(2)}) async-start(f32[3,1536,8,192]{3,2,0,1:T(8,128)} %pad_maximum_fusion), calls=%async_computation.2 | async-start | bytes 75497472 | tf_op jit(solution)/shard_map/all_to_all | solution.py:47
  1053.7 6.2 copy-start.2
  1053.7 13.5 slice-start.9
  1055.1 12.1 copy-start.1
  1059.9 7.3 slice-start.10
where the time goes:
time: 2390 us; the launch traced here: 2380 us
  blocking collectives  999 us (42%)
  waiting for transfers between devices  633 us (26%)
  local copies, waits for them, and re-layouts  441 us (18%)
  other arithmetic  166 us (7%)
  matrix products  131 us (5%)
    all_to_all x1, waiting for transfers between devices, body(): lax.all_to_all(span_terms(span_lines, span_operator), 'col', split_axis=1...  633 us
    all_to_all x1, blocking collectives, body(): lax.all_to_all(combined, 'row', split_axis=3, concat_axis=2, tiled=True)  427 us
    all_to_all x1, blocking collectives, body(): lax.all_to_all(wall_lines, 'col', split_axis=3, concat_axis=1, tiled=True)  414 us
    all_to_all x1, blocking collectives, body(): lax.all_to_all(truncated_outcome, 'row', split_axis=2, concat_axis=3, til...  158 us
    another operation x3, other arithmetic, skew_terms(): jnp.stack([0.5 * (slope_list[3 + index] + speed_field_holder * slope_list...  80.7 us
    dot_general x6, matrix products, span_terms(): jnp.dot(span_operator, field, preferred_element_type=jnp.float32)  80.3 us
    all_to_all x1, local copies, waits for them, and re-layouts, body(): lax.all_to_all(wall_lines, 'col', split_axis=3, concat_axis=1, tiled=True)  76.6 us
    another operation x4, local copies, waits for them, and re-layouts, skew_terms(): jnp.stack([0.5 * (slope_list[3 + index] + speed_field_holder * slope_list...  75.8 us
  transfers between devices with their start and end apart: 1, of which 1 were waited for; matrix products, arithmetic and copies ran while one was open for 7% of the time, Pallas kernels for 0%

commit v1 on v0

v1 whole, which is shorter than its diff:
```python
import functools

import jax
import jax.numpy as jnp
from jax import lax
from jax.experimental import pallas as pl
from jax.experimental.pallas import tpu as pltpu
from jax.sharding import PartitionSpec as P

MESH = pl.DeviceIdType.MESH


def exchange_kernel(
    nrow, ncol, yl,
    lines, wall_t, span_op,
    row_in, col_in, wall_back, span_back,
    wslot, lhs, wout, sslot, prod, sout,
    row_send, row_recv, col_send, col_recv, wb_send, wb_recv, sb_send, sb_recv, load_sem,
):
    my_row, my_col = lax.axis_index("row"), lax.axis_index("col")
    xs, zl = lines.shape[0], lines.shape[1]
    nz = span_op.shape[0]
    pr, pc = xs // nrow, xs // ncol
    f32, bf16 = jnp.float32, jnp.bfloat16

    def row_peer(k):
        return lax.rem(my_row + k, nrow)

    def col_peer(k):
        return lax.rem(my_col + k, ncol)

    def zrows(index):
        return pl.ds(pl.multiple_of(index * zl, 16), zl)

    def move(src, dst, send, recv, axis, k):
        if k == 0:
            return pltpu.make_async_copy(src, dst, recv)
        peer = row_peer(k) if axis == "row" else col_peer(k)
        return pltpu.make_async_remote_copy(
            src_ref=src, dst_ref=dst, send_sem=send, recv_sem=recv,
            device_id={axis: peer}, device_id_type=MESH,
        )

    def row_copy(p, k):
        return move(
            lines.at[row_peer(k) * pr + p], row_in.at[p, my_row],
            row_send.at[p, k], row_recv.at[p, k], "row", k,
        )

    def col_copy(p, k):
        return move(
            lines.at[col_peer(k) * pc + p], col_in.at[p, zrows(my_col)],
            col_send.at[p, k], col_recv.at[p, k], "col", k,
        )

    def wall_copy(p, k):
        return move(
            wout.at[p, row_peer(k)], wall_back.at[my_row * pr + p],
            wb_send.at[p, k], wb_recv.at[p, k], "row", k,
        )

    def span_copy(p, k):
        return move(
            sout.at[p, zrows(col_peer(k))], span_back.at[my_col * pc + p],
            sb_send.at[p, k], sb_recv.at[p, k], "col", k,
        )

    def arrived(copy, k):
        if k == 0:
            copy.wait()
        else:
            copy.wait_recv()

    barrier = pltpu.get_barrier_semaphore()
    for k in range(1, nrow):
        pl.semaphore_signal(barrier, inc=1, device_id={"row": row_peer(k)}, device_id_type=MESH)
    for k in range(1, ncol):
        pl.semaphore_signal(barrier, inc=1, device_id={"col": col_peer(k)}, device_id_type=MESH)
    pl.semaphore_wait(barrier, nrow + ncol - 2)

    per = pr // pc

    def launch(i, carry):
        for k in list(range(1, ncol)) + [0]:
            col_copy(i, k).start()

        def launch_row(j, inner):
            for k in list(range(1, nrow)) + [0]:
                row_copy(i * per + j, k).start()
            return inner

        return lax.fori_loop(0, per, launch_row, carry)

    lax.fori_loop(0, pc, launch, 0)

    def wall_plane(p):
        for k in range(nrow):
            arrived(row_copy(p, k), k)
        load = pltpu.make_async_copy(row_in.at[p], wslot, load_sem.at[0])
        load.start()
        load.wait()
        for b in range(nrow):
            speed = wslot[b, :, yl : 2 * yl].astype(f32)
            for c in range(3):
                field = wslot[b, :, c * yl : (c + 1) * yl]
                lhs[c, :zl, b * yl : (b + 1) * yl] = field
                lhs[c, zl:, b * yl : (b + 1) * yl] = (field.astype(f32) * speed).astype(bf16)

        def component(c, carry):
            for h in range(0, nrow, 2):
                acc = jnp.dot(
                    lhs[c], wall_t[:, h * yl : (h + 2) * yl], preferred_element_type=f32
                )
                for b in (0, 1):
                    speed = wslot[h + b, :, yl : 2 * yl].astype(f32)
                    part = acc[:, b * yl : (b + 1) * yl]
                    wout[p, h + b, :, pl.ds(pl.multiple_of(c * yl, 128), yl)] = (
                        0.5 * (part[zl:] + speed * part[:zl])
                    ).astype(bf16)
            return carry

        lax.fori_loop(0, 3, component, 0)
        for k in list(range(1, nrow)) + [0]:
            wall_copy(p, k).start()

    tile = nz // 4

    def span_plane(p):
        for k in range(ncol):
            arrived(col_copy(p, k), k)
        load = pltpu.make_async_copy(col_in.at[p], sslot, load_sem.at[1])
        load.start()
        load.wait()

        def products(t, carry):
            rows = pl.ds(pl.multiple_of(t * tile, 16), tile)
            speed = sslot[rows, 2 * yl : 3 * yl].astype(f32)
            for c in range(3):
                cells = slice(c * yl, (c + 1) * yl)
                prod[rows, cells] = (sslot[rows, cells].astype(f32) * speed).astype(bf16)
            return carry

        lax.fori_loop(0, 4, products, 0)

        def outputs(t, carry):
            rows = pl.ds(pl.multiple_of(t * tile, 16), tile)
            speed = sslot[rows, 2 * yl : 3 * yl].astype(f32)
            first = jnp.dot(span_op[rows, :], sslot[...], preferred_element_type=f32)
            second = jnp.dot(span_op[rows, :], prod[...], preferred_element_type=f32)
            for c in range(3):
                cells = slice(c * yl, (c + 1) * yl)
                sout[p, rows, cells] = (0.5 * (second[:, cells] + speed * first[:, cells])).astype(bf16)
            return carry

        lax.fori_loop(0, 4, outputs, 0)
        for k in list(range(1, ncol)) + [0]:
            span_copy(p, k).start()

    def work(i, carry):
        def wall_step(j, inner):
            wall_plane(i * per + j)
            return inner

        lax.fori_loop(0, per, wall_step, 0)
        span_plane(i)
        return carry

    lax.fori_loop(0, pc, work, 0)

    def finish_row(p, carry):
        for k in range(nrow):
            arrived(wall_copy(p, k), k)
            if k:
                wall_copy(p, k).wait_send()
                row_copy(p, k).wait_send()
        return carry

    def finish_col(p, carry):
        for k in range(ncol):
            arrived(span_copy(p, k), k)
            if k:
                span_copy(p, k).wait_send()
                col_copy(p, k).wait_send()
        return carry

    lax.fori_loop(0, pr, finish_row, 0)
    lax.fori_loop(0, pc, finish_col, 0)


def body(nrow, ncol, velocity, wall_operator, span_operator):
    _, zl, xs, yl = velocity.shape
    ny, nz = wall_operator.shape[0], span_operator.shape[0]
    pr, pc = xs // nrow, xs // ncol
    bf16 = jnp.bfloat16
    lines = velocity.astype(bf16).transpose(2, 1, 0, 3).reshape(xs, zl, 3 * yl)
    dma = pltpu.SemaphoreType.DMA
    anywhere = pl.BlockSpec(memory_space=pl.ANY)
    vmem = pl.BlockSpec(memory_space=pltpu.VMEM)
    flops = 2 * 6 * zl * pr * ny * ny + 2 * 6 * nz * pc * yl * nz
    _, _, wall_back, span_back = pl.pallas_call(
        functools.partial(exchange_kernel, nrow, ncol, yl),
        out_shape=[
            jax.ShapeDtypeStruct((pr, nrow, zl, 3 * yl), bf16),
            jax.ShapeDtypeStruct((pc, nz, 3 * yl), bf16),
            jax.ShapeDtypeStruct((xs, zl, 3 * yl), bf16),
            jax.ShapeDtypeStruct((xs, zl, 3 * yl), bf16),
        ],
        in_specs=[anywhere, vmem, vmem],
        out_specs=[anywhere] * 4,
        scratch_shapes=[
            pltpu.VMEM((nrow, zl, 3 * yl), bf16),
            pltpu.VMEM((3, 2 * zl, ny), bf16),
            pltpu.VMEM((pr, nrow, zl, 3 * yl), bf16),
            pltpu.VMEM((nz, 3 * yl), bf16),
            pltpu.VMEM((nz, 3 * yl), bf16),
            pltpu.VMEM((pc, nz, 3 * yl), bf16),
            dma((pr, nrow)), dma((pr, nrow)),
            dma((pc, ncol)), dma((pc, ncol)),
            dma((pr, nrow)), dma((pr, nrow)),
            dma((pc, ncol)), dma((pc, ncol)),
            dma((2,)),
        ],
        compiler_params=pltpu.CompilerParams(
            collective_id=0, has_side_effects=True, vmem_limit_bytes=60 * 2**20
        ),
        cost_estimate=pl.CostEstimate(
            flops=flops, bytes_accessed=8 * xs * zl * 3 * yl * 2, transcendentals=0
        ),
    )(lines, wall_operator.T, span_operator)
    total = wall_back.astype(jnp.float32) + span_back.astype(jnp.float32)
    return total.reshape(xs, zl, 3, yl).transpose(2, 1, 0, 3)


def solution(mesh):
    placed = (P(None, "col", None, "row"), P(), P())
    return jax.shard_map(
        functools.partial(body, mesh.shape["row"], mesh.shape["col"]),
        mesh=mesh, in_specs=placed, out_specs=P(None, "col", None, "row"), check_vma=False,
    )
```

time: 2390 us -> 822 us (0.34)
  blocking collectives: 999 us -> 0 us
  waiting for transfers between devices: 633 us -> 0 us
  Pallas kernels: 0 us -> 620 us
  local copies, waits for them, and re-layouts: 441 us -> 169 us
  other arithmetic: 166 us -> 31 us
  matrix products: 131 us -> 0 us
    all_to_all x3 -> x0, blocking collectives: 999 us -> none  [the longest x1 427 us: body(): lax.all_to_all(combined, 'row', split_axis=3, concat_axis=2, tiled=True)]
    all_to_all x1 -> x0, waiting for transfers between devices: 633 us -> none  [body(): lax.all_to_all(span_terms(span_lines, span_operator), 'col', split_axis=1...]
    pallas_call x0 -> x1, Pallas kernels: none -> 620 us  [body(): pl.pallas_call(functools.partial(exchange_kernel, nrow, ncol, yl), out_sh...]
    all_to_all x5 -> x0, local copies, waits for them, and re-layouts: 197 us -> none  [the longest x1 76.6 us: body(): lax.all_to_all(wall_lines, 'col', split_axis=3, concat_axis=1, tiled=True)]
    dot_general x7 -> x0, matrix products: 131 us -> none  [the longest x6 80.3 us: span_terms(): jnp.dot(span_operator, field, preferred_element_type=jnp.float32)]
    transpose x0 -> x2, local copies, waits for them, and re-layouts: none -> 87.3 us  [the longest x1 58 us: body(): lines = velocity.astype(bf16).transpose(2, 1, 0, 3).reshape(xs, zl, 3 * yl)]
    convert_element_type x3 -> x0, local copies, waits for them, and re-layouts: 80.8 us -> none  [the longest x2 73.3 us: span_terms(): merged.astype(jnp.float32) * speed_field_holder]
    another operation x3 -> x0, other arithmetic: 80.7 us -> none  [skew_terms(): jnp.stack([0.5 * (slope_list[3 + index] + speed_field_holder * slope_list...]
  transfers between devices with their start and end apart: 1 -> 0, of which waited for: 1 -> 0; matrix products, arithmetic and copies ran while one was open for 7% -> 0% of each run, Pallas kernels for 0% -> 0%
where the time goes in v1:
time: 822 us; the launch traced here: 819 us
  Pallas kernels  620 us (75%)
  local copies, waits for them, and re-layouts  169 us (21%)
  other arithmetic  31 us (4%)
    pallas_call x1, Pallas kernels, body(): pl.pallas_call(functools.partial(exchange_kernel, nrow, ncol, yl), out_sh...  620 us
    transpose x1, local copies, waits for them, and re-layouts, body(): lines = velocity.astype(bf16).transpose(2, 1, 0, 3).reshape(xs, zl, 3 * yl)  58 us
    reshape x1, local copies, waits for them, and re-layouts, body(): return total.reshape(xs, zl, 3, yl).transpose(2, 1, 0, 3)  40.2 us
    reshape x1, local copies, waits for them, and re-layouts, body(): lines = velocity.astype(bf16).transpose(2, 1, 0, 3).reshape(xs, zl, 3 * yl)  34.7 us
    transpose x1, local copies, waits for them, and re-layouts, body(): return total.reshape(xs, zl, 3, yl).transpose(2, 1, 0, 3)  29.3 us
    add x1, other arithmetic, body(): total = wall_back.astype(jnp.float32) + span_back.astype(jnp.float32)  20.4 us

profile of v1, /device:TPU:30, one launch (start us, length us, event | category | flops | bytes accessed | tf_op | source)
XLA Modules:
  0.0 819.4 jit_solution(10208112052265162196)
XLA Ops:
  0.0 6.7 copy.8
  6.7 10.5 %convert_bitcast_fusion = bf16[32,192,3,384]{3,0,1,2:T(8,128)(2,1)S(1)} fusion(f32[3,192,32,384]{3,2,1,0:T(8,128)} %param.3), kind=kLoop, calls=%fused_computation.1 | loop fusion | flops 7077888 | bytes 42467328 | tf_op jit(solution)/shard_map/transpose | solution.py:195
  17.2 58.0 %copy.7 = bf16[32,192,3,384]{3,2,1,0:T(4,128)(2,1)} copy(bf16[32,192,3,384]{3,0,1,2:T(8,128)(2,1)S(1)} %convert_bitcast_fusion) | data formatting | bytes 28311552 | tf_op jit(solution)/shard_map/transpose | solution.py:195
  75.2 34.7 %reshape.6.lines = bf16[32,192,1152]{2,1,0:T(8,128)(2,1)} reshape(bf16[32,192,3,384]{3,2,1,0:T(4,128)(2,1)} %copy.7) | data formatting | bytes 28311552 | tf_op jit(solution)/shard_map/reshape | solution.py:195
  109.9 619.5 %shard_map.37 = (bf16[8,4,192,1152]{3,2,1,0:T(8,128)(2,1)}, bf16[4,1536,1152]{2,1,0:T(8,128)(2,1)}, bf16[32,192,1152]{2,1,0:T(8,128)(2,1)}, bf16[32,192,1152]{2,1,0:T(8,128)(2,1)}) custom-call(bf16[32,192,1152]{2,1,0:T(8,128)(2,1)} %reshape.6.lines, bf16[1536,1536]{1,0:T(8,128)(2,1)} %bitcast.5, bf16[1536,1536]{1,0:T(8,128)(2,1)} %span_op.1), custom_call_target="tpu_custom_call" | custom-call | flops 86973087744 | bytes 113246208 | tf_op jit(solution)/shard_map/pallas_call | solution.py:200
  729.5 20.4 %convert_add_fusion = f32[32,192,1152]{2,1,0:T(8,128)} fusion(bf16[32,192,1152]{2,1,0:T(8,128)(2,1)} %get-tuple-element.8, bf16[32,192,1152]{2,1,0:T(8,128)(2,1)} %get-tuple-element.7), kind=kLoop, calls=%fused_computation | loop fusion | flops 21233664 | bytes 56623104 | tf_op jit(solution)/shard_map/add | solution.py:230
  749.9 40.2 %reshape.7 = f32[32,192,3,384]{3,2,1,0:T(4,128)} reshape(f32[32,192,1152]{2,1,0:T(8,128)} %convert_add_fusion) | data formatting | bytes 56623104 | tf_op jit(solution)/shard_map/reshape | solution.py:231
  790.1 29.3 %copy.9 = f32[3,192,32,384]{3,2,1,0:T(8,128)} copy(f32[3,192,32,384]{3,0,1,2:T(4,128)} %bitcast.4) | data formatting | bytes 56623104 | tf_op jit(solution)/shard_map/transpose | solution.py:231
